TPU v7x, 256 devices: a whole 4x4x8 slice. The times are simulated.
256 devices in a mesh: cuts: 16 (over z, y_hi), loop: 16 (over y_lo, x, core).
Axes of the slice: x: 4, y: 4 (y_hi: 2, y_lo: 2; y = y_hi * 2 + y_lo), z: 8, core: 2. Of those that a mesh axis runs over, the one named last changes fastest.
Arguments:
- image_features: bfloat16 [65536, 1152], P(('cuts', 'loop')), may hold values from -0.1796875 to 0.1796875
- text_features: bfloat16 [65536, 1152], P(('cuts', 'loop')), may hold values from -0.1796875 to 0.1796875
- image_head: bfloat16 [1152, 1152], replicated, may hold values from -0.1875 to 0.1875
- text_head: bfloat16 [1152, 1152], replicated, may hold values from -0.1875 to 0.1875
Outputs:
- image_grad: float32 [65536, 1152], P(('cuts', 'loop'))
- text_grad: float32 [65536, 1152], P(('cuts', 'loop'))
- image_head_grad: float32 [1152, 1152], P('loop')
- text_head_grad: float32 [1152, 1152], P('loop')
All inputs are finite; a program needn't handle non-finite values.
Results may differ from a plain program's by a relative error of at most 0.024.
Values may be sent and summed in bfloat16 or wider, within the bound.
A program may use at most 128 MiB of HBM per device.

v0:
```python
import jax
import jax.numpy as jnp
from jax import lax
from jax.sharding import PartitionSpec as P

SCORE_SCALE = 10.0
SCORE_BIAS = -2.5
EPSILON = 1e-06


def normalize(features, weight_matrix):
    projected = jnp.dot(features, weight_matrix, preferred_element_type=jnp.float32)
    factor = lax.rsqrt(jnp.sum(projected * projected, axis=-1, keepdims=True) + EPSILON)
    return (projected * factor, factor)


def pair_weights(image_vectors, text_vectors, image_offset):
    pair_scores = (
        SCORE_SCALE
        * lax.dot_general(
            image_vectors,
            text_vectors,
            (((1,), (1,)), ((), ())),
            preferred_element_type=jnp.float32,
        )
        + SCORE_BIAS
    )
    row_ids = image_offset + lax.broadcasted_iota(jnp.int32, pair_scores.shape, 0)
    col_ids = lax.broadcasted_iota(jnp.int32, pair_scores.shape, 1)
    match_targets = jnp.where(row_ids == col_ids, 1.0, -1.0).astype(jnp.float32)
    return (SCORE_SCALE * -match_targets * jax.nn.sigmoid(-match_targets * pair_scores)).astype(
        jnp.bfloat16
    )


def norm_back(unit, factor, gradient):
    return (factor * (gradient - unit * jnp.sum(unit * gradient, axis=-1, keepdims=True))).astype(
        jnp.bfloat16
    )


def contract_rows(left, right):
    return lax.dot_general(
        left, right, (((0,), (0,)), ((), ())), preferred_element_type=jnp.float32
    )


def per_device(image_features, text_features, image_head, text_head):
    row_count = image_features.shape[0]
    my_place = lax.axis_index("loop")
    own_start = my_place * row_count
    image_unit, image_factor = normalize(image_features, image_head)
    text_unit, text_factor = normalize(text_features, text_head)
    image_vectors = image_unit.astype(jnp.bfloat16)
    text_vectors = text_unit.astype(jnp.bfloat16)
    arrived = lax.all_gather(text_vectors, "loop", axis=0, tiled=True)
    weights = pair_weights(image_vectors, arrived, own_start)
    summed = jnp.dot(weights, arrived, preferred_element_type=jnp.float32)
    text_attraction = lax.psum_scatter(
        contract_rows(weights, image_vectors).astype(jnp.bfloat16),
        "loop",
        scatter_dimension=0,
        tiled=True,
    ).astype(jnp.float32)
    image_back = norm_back(image_unit, image_factor, summed)
    text_back = norm_back(text_unit, text_factor, text_attraction)
    image_grad = lax.dot_general(
        image_back, image_head, (((1,), (1,)), ((), ())), preferred_element_type=jnp.float32
    )
    text_grad = lax.dot_general(
        text_back, text_head, (((1,), (1,)), ((), ())), preferred_element_type=jnp.float32
    )
    image_wgrad = contract_rows(image_features, image_back).astype(jnp.bfloat16)
    text_wgrad = contract_rows(text_features, text_back).astype(jnp.bfloat16)
    image_part, text_part = (
        lax.psum_scatter(image_wgrad, "loop", scatter_dimension=0, tiled=True).astype(jnp.float32),
        lax.psum_scatter(text_wgrad, "loop", scatter_dimension=0, tiled=True).astype(jnp.float32),
    )
    image_head_grad, text_head_grad = (
        lax.psum(image_part.astype(jnp.bfloat16), "cuts").astype(jnp.float32),
        lax.psum(text_part.astype(jnp.bfloat16), "cuts").astype(jnp.float32),
    )
    return (image_grad, text_grad, image_head_grad, text_head_grad)


def solution(mesh):
    placed = (P(("cuts", "loop"), None), P(("cuts", "loop"), None), P(), P())
    return jax.shard_map(
        per_device,
        mesh=mesh,
        in_specs=placed,
        out_specs=(
            P(("cuts", "loop"), None),
            P(("cuts", "loop"), None),
            P("loop", None),
            P("loop", None),
        ),
        check_vma=False,
    )
```

profile of v0, /device:TPU:1, one launch (start us, length us, event | category | flops | bytes accessed | tf_op | source)
XLA Modules:
  0.0 477.0 jit_solution(14657469178935727883)
XLA Ops:
  7.2 0.0 all-gather.2.cloned.1.call-start
  7.2 3.2 multiply_reduce_fusion.1
  10.4 1.0 copy-done.1
  11.4 1.0 multiply_convert_fusion.1
  12.4 0.0 reduce-scatter.4.cloned.1.call-start
  12.5 2.0 multiply_reduce_fusion.2
  14.5 61.9 %all-gather.2.cloned.1.call-done = bf16[4096,1152]{1,0:T(8,128)(2,1)} async-done(((bf16[256,1152]{1,0:T(8,128)(2,1)}), bf16[4096,1152]{1,0:T(8,128)(2,1)}) %all-gather.2.cloned.1.call-update) | async-done | bytes 9437200 | tf_op jit(solution)/shard_map/all_gather | solution.py:56
  76.3 7.9 %fusion.9 = bf16[256,4096]{1,0:T(8,128)(2,1)S(1)} fusion(bf16[4096,1152]{1,0:T(8,128)(2,1)} %all-gather.2.cloned.1.call-done, s32[256]{0:T(256)S(1)} %iota_add_fusion, f32[256,1152]{1,0:T(8,128)} %get-tuple-element.19, f32[256]{0:T(256)S(1)} %add_rsqrt_fusion.1), kind=kOutput, calls=%fused_computation.13 | convolution fusion | flops 2429091840 | bytes 12716032 | tf_op jit(solution)/shard_map/dot_general | solution.py:20
  84.3 1.3 copy-done.6
  85.6 5.4 %convolution_convert_fusion = bf16[4096,1152]{1,0:T(8,128)(2,1)} fusion(bf16[256,4096]{1,0:T(8,128)(2,1)S(1)} %fusion.9, f32[256,1152]{1,0:T(8,128)S(1)} %copy-done.3, f32[256]{0:T(256)S(1)} %add_rsqrt_fusion.1), kind=kOutput, calls=%fused_computation | convolution fusion | flops 2421227520 | bytes 12715008 | tf_op jit(solution)/shard_map/dot_general | solution.py:43
  91.0 0.0 reduce-scatter.4.cloned.1.call-update
  91.0 0.2 all-reduce.7.cloned.1.call-start
  91.2 7.6 %multiply_reduce_fusion = (f32[256]{0:T(256)S(1)}, f32[256,1152]{1,0:T(8,128)S(1)}) fusion(f32[256,1152]{1,0:T(8,128)} %get-tuple-element.19, f32[256]{0:T(256)S(1)} %add_rsqrt_fusion.1, bf16[256,4096]{1,0:T(8,128)(2,1)} %copy-done.6, bf16[4096,1152]{1,0:T(8,128)(2,1)} %all-gather.2.cloned.1.call-done), kind=kOutput, calls=%fused_computation.21 | convolution fusion | flops 2416803584 | bytes 13895680 | tf_op jit(solution)/shard_map/dot_general | solution.py:58
  98.9 0.2 multiply_convert_fusion
  99.1 0.8 copy-done.9
  99.9 2.5 fusion
  102.4 65.3 %reduce-scatter.4.cloned.1.call-done = bf16[256,1152]{1,0:T(8,128)(2,1)} async-done(((bf16[4096,1152]{1,0:T(8,128)(2,1)}), bf16[256,1152]{1,0:T(8,128)(2,1)}) %reduce-scatter.4.cloned.1.call-update) | async-done | bytes 589840 | tf_op jit(solution)/shard_map/reduce_scatter | solution.py:59
  167.7 1.9 fusion.10
  169.6 0.0 copy-done.7
  169.7 0.3 fusion.12
  170.0 0.8 copy-done.5
  170.8 2.6 fusion.1
  173.4 0.0 all-reduce.9.cloned.1.call-start
  173.4 0.6 copy-done.11
  174.0 0.6 dynamic-slice
  175.2 2.0 fusion.13
  177.3 135.8 %all-reduce.7.cloned.1.call-done = (bf16[1152,1152]{0,1:T(8,128)(2,1)}, bf16[1152,1152]{0,1:T(8,128)(2,1)}) async-done(((bf16[1152,1152]{0,1:T(8,128)(2,1)}, bf16[1152,1152]{0,1:T(8,128)(2,1)}), (bf16[1152,1152]{0,1:T(8,128)(2,1)}, bf16[1152,1152]{0,1:T(8,128)(2,1)})) %all-reduce.7.cloned.1.call-update) | async-done | bytes 5308432
  313.1 2.3 constant_dynamic-slice_fusion
  315.4 4.0 fusion.14
  319.4 147.4 %all-reduce.9.cloned.1.call-done = (bf16[72,1152]{0,1:T(8,128)(2,1)}, bf16[72,1152]{0,1:T(8,128)(2,1)}) async-done(((bf16[72,1152]{0,1:T(8,128)(2,1)}, bf16[72,1152]{0,1:T(8,128)(2,1)}), (bf16[72,1152]{0,1:T(8,128)(2,1)}, bf16[72,1152]{0,1:T(8,128)(2,1)})) %all-reduce.9.cloned.1.call-update) | async-done | bytes 331792 | tf_op jit(solution)/shard_map/psum | solution.py:80
  466.8 1.8 copy.10
  468.6 1.8 copy.11
  (24 shorter events, 0.1 us)
Async XLA Ops:
  7.2 5.3 %copy-start = (bf16[1152,1152]{1,0:T(8,128)(2,1)S(1)}, bf16[1152,1152]{1,0:T(8,128)(2,1)}, u32[]{:S(2)}) copy-start(bf16[1152,1152]{1,0:T(8,128)(2,1)} %param.6) | copy-start | bytes 7962628
  7.2 69.2 %all-gather.2.cloned.1.call-start = ((), (), s32[]{:S(2)}) async-start(), calls=%async_computation.1 | async-start | bytes 10027008 | tf_op jit(solution)/shard_map/all_gather | solution.py:56
  10.4 1.0 copy-start.1
  10.4 2.1 copy-start.8
  12.4 155.3 %reduce-scatter.4.cloned.1.call-start = ((), (), s32[]{:S(2)}) async-start(), calls=%async_computation.2 | async-start | bytes 10027008 | tf_op jit(solution)/shard_map/reduce_scatter | solution.py:59
  76.3 9.2 %copy-start.3 = (f32[256,1152]{1,0:T(8,128)S(1)}, f32[256,1152]{1,0:T(8,128)}, u32[]{:S(2)}) copy-start(f32[256,1152]{1,0:T(8,128)} %get-tuple-element.19) | copy-start | bytes 3538948
  84.3 1.3 copy-start.6
  91.0 222.1 %all-reduce.7.cloned.1.call-start = ((), (), s32[]{:S(2)}) async-start(), calls=%async_computation.3 | async-start | bytes 10616832
  91.2 7.6 %copy-start.4 = (f32[256,1152]{1,0:T(8,128)S(1)}, f32[256,1152]{1,0:T(8,128)}, u32[]{:S(2)}) copy-start(f32[256,1152]{1,0:T(8,128)} %get-tuple-element.19) | copy-start | bytes 3538948
  98.8 1.1 copy-start.9
  167.7 1.9 copy-start.2
  167.7 1.9 copy-start.7
  167.7 3.1 copy-start.10
  169.9 0.8 copy-start.5
  173.3 0.7 copy-start.11
  173.4 293.4 %all-reduce.9.cloned.1.call-start = ((), (), s32[]{:S(2)}) async-start(), calls=%async_computation.4 | async-start | bytes 1179648 | tf_op jit(solution)/shard_map/psum | solution.py:80
Sparse Core Ops, SparseCore 0:
  12.5 63.7 all-gather.1
  91.1 76.5 reduce-scatter.3
  173.5 139.5 all-reduce.6
  316.2 150.4 all-reduce.8
where the time goes:
time: 487 us; the launch traced here: 477 us
  waiting for transfers between devices  410 us (84%)
  matrix products  37.2 us (8%)
  between operations  14.6 us (3%)
  local copies, waits for them, and re-layouts  11.2 us (2%)
    psum x1, waiting for transfers between devices, per_device(): lax.psum(image_part.astype(jnp.bfloat16), 'cuts').astype(jnp.float32)  147 us
    unnamed x5, waiting for transfers between devices  136 us
    reduce_scatter x1, waiting for transfers between devices, per_device(): lax.psum_scatter(contract_rows(weights, image_vectors).astype(jnp.bfloat1...  65.3 us
    all_gather x1, waiting for transfers between devices, per_device(): arrived = lax.all_gather(text_vectors, 'loop', axis=0, tiled=True)  61.9 us
    unnamed x28, local copies, waits for them, and re-layouts  11.2 us
    dot_general x3, matrix products, contract_rows(): lax.dot_general(left, right, (((0,), (0,)), ((), ())), preferred_element_...  10.5 us
  transfers between devices with their start and end apart: 4, of which 4 were waited for; matrix products, arithmetic and copies ran while one was open for 4% of the time, Pallas kernels for 0%

commit v1 on v0

v1 whole, which is shorter than its diff:
```python
import jax
import jax.numpy as jnp
from jax import lax
from jax.experimental import pallas as pl
from jax.experimental.pallas import tpu as pltpu
from jax.sharding import PartitionSpec as P

SCORE_SCALE = 10.0
SCORE_BIAS = -2.5
EPSILON = 1e-06

D = 1152
B = 256
HB = 128
NZ, NY, NX = 8, 4, 4
BLK = 8
BR = D // BLK
RT, CT = BR // 16, D // 128
NT = RT * CT
ZT = 11
TP = ZT * NZ
F32, BF16 = jnp.float32, jnp.bfloat16
MESH = pl.DeviceIdType.MESH


def kernel(
    fi_hbm, ft_hbm, hi_hbm, ht_hbm,
    gi_out, gt_out, wi_out, wt_out,
    fi, ft, hi, ht, x32, xb, sx, y32, yb, sy, w, wt, fit, ftt, g32, dpp, dqp,
    gsend, rx_opp, rx_l, rx_r, gysend, gyrecv, ysend, yrecv,
    tt, trecv, zh, zr, zs, pr, psum, zg, fin, finr,
    s_loc, s_fi, r_fi, s_ft, r_ft, s_yb, r_yb, s_gx, r_gx, s_gy, r_gy, s_y, r_y,
    s_t, r_t, s_z, r_z, s_p, r_p, s_g, r_g, s_f, r_f,
):
    cuts, loop = lax.axis_index("cuts"), lax.axis_index("loop")
    z, yh = cuts // 2, cuts % 2
    yl, x, core = loop // 8, (loop // 2) % 4, loop % 2
    me_plane = (yh * 2 + yl) * NX + x

    def dev(z_, yh_, yl_, x_, c_):
        return (z_ * 2 + yh_, (yl_ * NX + x_) * 2 + c_)

    right = dev(z, yh, yl, (x + 1) % NX, core)
    left = dev(z, yh, yl, (x + 3) % NX, core)
    mate = dev(z, yh, 1 - yl, x, core)
    sib = dev(z, yh, yl, x, 1 - core)
    zpeer = [dev((z + r) % NZ, yh, yl, x, core) for r in range(NZ)]
    up, down = zpeer[1], zpeer[7]

    def plane(r):
        q = (me_plane + r) % 16
        return dev(z, q // 8, (q // 4) % 2, q % 4, core), q % 8

    def local(src, dst, k):
        c = pltpu.make_async_copy(src, dst, s_loc.at[k])
        c.start()
        return c

    l_ft = local(ft_hbm, ft.at[0], 0)
    l_ht = local(ht_hbm, ht, 1)
    l_fi = local(fi_hbm, fi.at[0], 2)
    l_hi = local(hi_hbm, hi, 3)

    barrier = pltpu.get_barrier_semaphore()
    peers = [sib] + zpeer[1:] + [plane(r)[0] for r in range(1, 16)]
    for p in peers:
        pl.semaphore_signal(barrier, inc=1, device_id=p, device_id_type=MESH)
    pl.semaphore_wait(barrier, len(peers))

    def remote(src, dst, ss, rs, to):
        return pltpu.make_async_remote_copy(
            src_ref=src, dst_ref=dst, send_sem=ss, recv_sem=rs, device_id=to, device_id_type=MESH
        )

    A, Bh = pl.ds(0, HB), pl.ds(HB, HB)
    c_ra = remote(fi_hbm.at[A], fi.at[1, A], s_fi.at[0], r_fi.at[0], right)
    c_rb = remote(fi_hbm.at[Bh], fi.at[1, Bh], s_fi.at[1], r_fi.at[1], right)
    c_lb = remote(fi_hbm.at[Bh], fi.at[2, Bh], s_fi.at[2], r_fi.at[2], left)
    c_la = remote(fi_hbm.at[A], fi.at[2, A], s_fi.at[3], r_fi.at[3], left)
    c_ft = remote(ft_hbm, ft.at[1], s_ft.at[0], r_ft.at[0], mate)
    c_ra.start()
    c_lb.start()
    c_ft.start()
    c_rb.start()
    c_la.start()
    c_oa = remote(fi.at[1, A], fi.at[3, A], s_fi.at[4], r_fi.at[4], right)
    c_ob = remote(fi.at[2, Bh], fi.at[3, Bh], s_fi.at[5], r_fi.at[5], left)

    def normalize(f_ref, k, h_ref, v32, vb, s_ref):
        p = jnp.dot(f_ref[k], h_ref[...], preferred_element_type=F32)
        s = lax.rsqrt(jnp.sum(p * p, axis=-1, keepdims=True) + EPSILON)
        v = p * s
        v32[k] = v
        vb[k] = v.astype(BF16)
        s_ref[k] = s

    def flip(f_ref, k, t_ref):
        for j in range(CT):
            t_ref[pl.ds(j * 128, 128), pl.ds(k * B, B)] = f_ref[k, :, pl.ds(j * 128, 128)].T

    def weigh(i, j, own):
        sc = (
            SCORE_SCALE
            * lax.dot_general(xb[i], yb[j], (((1,), (1,)), ((), ())), preferred_element_type=F32)
            + SCORE_BIAS
        )
        half = (SCORE_SCALE * 0.5) * jnp.tanh(0.5 * sc)
        val = half + SCORE_SCALE * 0.5
        if own:
            same = lax.broadcasted_iota(jnp.int32, (B, B), 0) == lax.broadcasted_iota(
                jnp.int32, (B, B), 1
            )
            val = jnp.where(same, half - SCORE_SCALE * 0.5, val)
        w[i, :, pl.ds(j * B, B)] = val.astype(BF16)
        wt[j, :, pl.ds(i * B, B)] = val.T.astype(BF16)

    def pull(i):
        acc = jnp.dot(w[i, :, pl.ds(0, B)], yb[0], preferred_element_type=F32)
        for j in range(1, 4):
            acc += jnp.dot(w[i, :, pl.ds(j * B, B)], yb[j], preferred_element_type=F32)
        return acc

    def back(u, s, g):
        return (s * (g - u * jnp.sum(u * g, axis=-1, keepdims=True))).astype(BF16)

    c_yb = [remote(yb.at[k], yb.at[2 + k], s_yb.at[k], r_yb.at[k], sib) for k in range(2)]

    l_ft.wait()
    l_ht.wait()
    normalize(ft, 0, ht, y32, yb, sy)
    c_yb[0].start()
    l_fi.wait()
    l_hi.wait()
    normalize(fi, 0, hi, x32, xb, sx)
    weigh(0, 0, True)
    c_ra.wait_recv()
    c_oa.start()
    c_lb.wait_recv()
    c_ob.start()
    flip(fi, 0, fit)
    flip(ft, 0, ftt)
    c_yb[0].wait_recv()
    weigh(0, 2, False)
    c_ft.wait_recv()
    normalize(ft, 1, ht, y32, yb, sy)
    c_yb[1].start()
    c_rb.wait_recv()
    c_la.wait_recv()

    def neighbour(i, _):
        normalize(fi, i, hi, x32, xb, sx)
        return 0

    lax.fori_loop(1, 3, neighbour, 0)
    flip(ft, 1, ftt)
    flip(fi, 1, fit)
    flip(fi, 2, fit)
    weigh(0, 1, False)
    c_yb[1].wait_recv()
    weigh(0, 3, False)

    def tiles(k, _):
        weigh(1 + k // 4, k % 4, False)
        return 0

    lax.fori_loop(0, 8, tiles, 0)

    def image_pull(i, keep):
        g = pull(i)
        if keep is not None:
            keep[...] = g
        gsend[i] = g.astype(BF16)
        dpp[pl.ds(pl.multiple_of(i * B, B), B)] = back(x32[i], sx[i], g)

    def pull_neighbour(i, _):
        image_pull(i, g32.at[i - 1])
        return 0

    lax.fori_loop(1, 3, pull_neighbour, 0)
    c_nb = remote(gsend.at[2, Bh], rx_l.at[Bh], s_gx.at[0], r_gx.at[0], right)
    c_na = remote(gsend.at[1, A], rx_r.at[A], s_gx.at[1], r_gx.at[1], left)
    c_nb.start()
    c_na.start()
    image_pull(0, gi_out)

    c_oa.wait_recv()
    c_ob.wait_recv()
    normalize(fi, 3, hi, x32, xb, sx)

    def tiles_opp(k, _):
        weigh(3, k, False)
        return 0

    lax.fori_loop(0, 4, tiles_opp, 0)
    image_pull(3, None)
    c_pa = remote(gsend.at[3, A], rx_opp.at[A], s_gx.at[2], r_gx.at[2], right)
    c_pb = remote(gsend.at[3, Bh], rx_opp.at[Bh], s_gx.at[3], r_gx.at[3], left)
    c_pa.start()
    c_pb.start()
    flip(fi, 3, fit)

    def text_pull(j):
        acc = jnp.dot(wt[j, :, pl.ds(0, B)], xb[0], preferred_element_type=F32)
        for i in range(1, 4):
            acc += jnp.dot(wt[j, :, pl.ds(i * B, B)], xb[i], preferred_element_type=F32)
        return acc

    def for_sib(k, _):
        gysend[k] = text_pull(2 + k).astype(BF16)
        return 0

    lax.fori_loop(0, 2, for_sib, 0)
    c_gy = remote(gysend, gyrecv, s_gy, r_gy, sib)
    c_gy.start()

    g_mate = text_pull(1)
    gt_out[...] = text_pull(0)
    c_gy.wait_recv()
    g_mate += gyrecv[1].astype(F32)
    ysend[...] = g_mate.astype(BF16)
    c_y = remote(ysend, yrecv, s_y, r_y, mate)
    c_y.start()
    dqp[pl.ds(B, B)] = back(y32[1], sy[1], g_mate)
    g_own = gt_out[...] + gyrecv[0].astype(F32)
    gt_out[...] = g_own
    dqp[pl.ds(0, B)] = back(y32[0], sy[0], g_own)

    def head(f_t, d_ref, depth, slot):
        def row_block(b, _):
            o = jnp.dot(
                f_t[pl.ds(pl.multiple_of(b * BR, 16), BR), :], d_ref[...], preferred_element_type=F32
            ).astype(BF16)
            for r in range(RT):
                for c in range(CT):
                    tt[slot, b, c * RT + r] = o[r * 16 : r * 16 + 16, c * 128 : c * 128 + 128]
            return 0

        lax.fori_loop(0, BLK, row_block, 0)

    zero = jnp.zeros((BLK, TP - NT, 16, 128), BF16)
    tt[0, :, pl.ds(NT, TP - NT)] = zero
    tt[1, :, pl.ds(NT, TP - NT)] = zero
    c_t = remote(tt.at[1], trecv, s_t, r_t, sib)
    head(ftt, dqp, 2 * B, 1 - core)

    @pl.when(core == 0)
    def _():
        c_t.start()

    head(fit, dpp, 4 * B, core)

    @pl.when(core == 1)
    def _():
        c_t.start()

    c_pa.wait_recv()
    gsend[2, A] = (g32[1, A] + rx_opp[A].astype(F32)).astype(BF16)
    c_qa = remote(gsend.at[2, A], rx_l.at[A], s_gx.at[4], r_gx.at[4], right)
    c_qa.start()
    c_pb.wait_recv()
    gsend[1, Bh] = (g32[0, Bh] + rx_opp[Bh].astype(F32)).astype(BF16)
    c_qb = remote(gsend.at[1, Bh], rx_r.at[Bh], s_gx.at[5], r_gx.at[5], left)
    c_qb.start()

    c_t.wait_recv()

    def merge_t(b, _):
        tt[0, b] = (tt[0, b].astype(F32) + trecv[b].astype(F32)).astype(BF16)
        return 0

    lax.fori_loop(0, BLK, merge_t, 0)

    def piece(r):
        return pl.ds(ZT * ((z + r) % NZ), ZT)

    ZA = 6
    first_up = pl.ds(ZT * ((z + 4) % NZ), ZA)
    first_dn = pl.ds(ZT * ((z + 4) % NZ) + ZA, ZT - ZA)
    c_zu = remote(tt.at[0, :, first_up], zh.at[:, pl.ds(0, ZA)], s_z.at[0], r_z.at[0], up)
    c_zd = remote(tt.at[0, :, first_dn], zh.at[:, pl.ds(ZA, ZT - ZA)], s_z.at[1], r_z.at[1], down)
    c_zu.start()
    c_zd.start()
    sent = [c_zu, c_zd]
    for step in range(3):
        r = 3 - step
        c_zu.wait_recv()
        if step == 0:

            def add_up(b, _):
                zs[0, 0, b] = tt[0, b, piece(3)]
                zs[0, 0, b, pl.ds(0, ZA)] = (
                    tt[0, b, pl.ds(ZT * ((z + 3) % NZ), ZA)].astype(F32)
                    + zh[b, pl.ds(0, ZA)].astype(F32)
                ).astype(BF16)
                return 0

            def add_dn(b, _):
                zs[1, 0, b] = tt[0, b, piece(5)]
                zs[1, 0, b, pl.ds(ZA, ZT - ZA)] = (
                    tt[0, b, pl.ds(ZT * ((z + 5) % NZ) + ZA, ZT - ZA)].astype(F32)
                    + zh[b, pl.ds(ZA, ZT - ZA)].astype(F32)
                ).astype(BF16)
                return 0
        else:

            def add_up(b, _, step=step, r=r):
                zs[0, step, b] = (
                    tt[0, b, piece(r)].astype(F32) + zr[0, step - 1, b].astype(F32)
                ).astype(BF16)
                return 0

            def add_dn(b, _, step=step, r=r):
                zs[1, step, b] = (
                    tt[0, b, piece(8 - r)].astype(F32) + zr[1, step - 1, b].astype(F32)
                ).astype(BF16)
                return 0

        lax.fori_loop(0, BLK, add_up, 0)
        c_zu = remote(zs.at[0, step], zr.at[0, step], s_z.at[2 + 2 * step], r_z.at[2 + 2 * step], up)
        c_zu.start()
        c_zd.wait_recv()
        lax.fori_loop(0, BLK, add_dn, 0)
        c_zd = remote(
            zs.at[1, step], zr.at[1, step], s_z.at[3 + 2 * step], r_z.at[3 + 2 * step], down
        )
        c_zd.start()
        sent += [c_zu, c_zd]
        if step == 0:
            c_nb.wait_recv()
            c_na.wait_recv()
            c_qa.wait_recv()
            c_qb.wait_recv()
            dpf = back(x32[0], sx[0], gi_out[...] + rx_l[...].astype(F32) + rx_r[...].astype(F32))
            gi_out[...] = lax.dot_general(
                dpf, hi[...], (((1,), (1,)), ((), ())), preferred_element_type=F32
            )
        if step == 1:
            c_y.wait_recv()
            dqf = back(y32[0], sy[0], gt_out[...] + yrecv[...].astype(F32))
            gt_out[...] = lax.dot_general(
                dqf, ht[...], (((1,), (1,)), ((), ())), preferred_element_type=F32
            )
    c_zu.wait_recv()
    c_zd.wait_recv()

    def add_own(b, _):
        psum[b] = (
            tt[0, b, piece(0)].astype(F32) + zr[0, 2, b].astype(F32) + zr[1, 2, b].astype(F32)
        ).astype(BF16)
        return 0

    lax.fori_loop(0, BLK, add_own, 0)

    c_p = []
    for r in range(1, 16):
        to, blk = plane(r)
        c_p.append(remote(psum.at[blk], pr.at[r], s_p.at[r], r_p.at[r], to))
        c_p[-1].start()
    pr[0] = psum[me_plane % 8]
    for c in c_p:
        c.wait_recv()
    total = pr[me_plane].astype(F32)
    for q in range(1, 16):
        total += pr[(me_plane + 16 - q) % 16].astype(F32)
    zg[0] = total.astype(BF16)

    c_g = []
    for r in range(1, NZ):
        c_g.append(remote(zg.at[0], zg.at[r], s_g.at[r], r_g.at[r], zpeer[r]))
        c_g[-1].start()
    fin[pl.ds(ZT * z, ZT)] = zg[0]
    for r in range(1, NZ):
        c_g[r - 1].wait_recv()
        fin[pl.ds(ZT * ((z + 8 - r) % NZ), ZT)] = zg[r]
    c_f = remote(fin, finr, s_f, r_f, sib)
    c_f.start()
    c_f.wait_recv()

    def emit(ref, out, first):
        for c in range(CT):
            col = ref[pl.ds(c * RT, RT)].astype(F32).reshape(BR, 128)
            out[:, pl.ds(c * 128, 128)] = col[first : first + BR // 2]

    @pl.when(core == 0)
    def _():
        emit(fin, wi_out, 0)
        emit(finr, wt_out, 0)

    @pl.when(core == 1)
    def _():
        emit(finr, wi_out, BR // 2)
        emit(fin, wt_out, BR // 2)

    for c in (
        [c_ra, c_rb, c_lb, c_la, c_ft, c_oa, c_ob, c_nb, c_na, c_pa, c_pb, c_qa, c_qb, c_gy, c_y]
        + c_yb + [c_t, c_f] + sent + c_p + c_g
    ):
        c.wait_send()


def per_device(image_features, text_features, image_head, text_head):
    vm, dma = pltpu.VMEM, pltpu.SemaphoreType.DMA
    outs = (
        jax.ShapeDtypeStruct((B, D), F32),
        jax.ShapeDtypeStruct((B, D), F32),
        jax.ShapeDtypeStruct((BR // 2, D), F32),
        jax.ShapeDtypeStruct((BR // 2, D), F32),
    )
    return pl.pallas_call(
        kernel,
        out_shape=outs,
        in_specs=[pl.BlockSpec(memory_space=pl.ANY)] * 4,
        out_specs=[pl.BlockSpec(memory_space=pltpu.VMEM)] * 4,
        scratch_shapes=[
            vm((4, B, D), BF16), vm((2, B, D), BF16), vm((D, D), BF16), vm((D, D), BF16),
            vm((4, B, D), F32), vm((4, B, D), BF16), vm((4, B, 1), F32),
            vm((2, B, D), F32), vm((4, B, D), BF16), vm((2, B, 1), F32),
            vm((4, B, 4 * B), BF16), vm((4, B, 4 * B), BF16),
            vm((D, 4 * B), BF16), vm((D, 2 * B), BF16),
            vm((2, B, D), F32), vm((4 * B, D), BF16), vm((2 * B, D), BF16),
            vm((4, B, D), BF16), vm((B, D), BF16),
            vm((B, D), BF16), vm((B, D), BF16),
            vm((2, B, D), BF16), vm((2, B, D), BF16),
            vm((B, D), BF16), vm((B, D), BF16),
            vm((2, BLK, TP, 16, 128), BF16), vm((BLK, TP, 16, 128), BF16),
            vm((BLK, ZT, 16, 128), BF16), vm((2, 3, BLK, ZT, 16, 128), BF16),
            vm((2, 3, BLK, ZT, 16, 128), BF16), vm((16, ZT, 16, 128), BF16),
            vm((BLK, ZT, 16, 128), BF16), vm((NZ, ZT, 16, 128), BF16),
            vm((TP, 16, 128), BF16), vm((TP, 16, 128), BF16),
            dma((4,)), dma((6,)), dma((6,)), dma((1,)), dma((1,)), dma((2,)), dma((2,)),
            dma((6,)), dma((6,)), dma(()), dma(()), dma(()), dma(()),
            dma(()), dma(()), dma((8,)), dma((8,)), dma((16,)), dma((16,)),
            dma((8,)), dma((8,)), dma(()), dma(()),
        ],
        compiler_params=pltpu.CompilerParams(
            collective_id=0, has_side_effects=True, vmem_limit_bytes=63 << 20
        ),
        name="siglip_back",
    )(image_features, text_features, image_head, text_head)


def solution(mesh):
    placed = (P(("cuts", "loop"), None), P(("cuts", "loop"), None), P(), P())
    return jax.shard_map(
        per_device,
        mesh=mesh,
        in_specs=placed,
        out_specs=(
            P(("cuts", "loop"), None),
            P(("cuts", "loop"), None),
            P("loop", None),
            P("loop", None),
        ),
        check_vma=False,
    )
```

time: 487 us -> 119 us (0.24); the launches traced: 477 us -> 119 us
  waiting for transfers between devices: 410 us -> 0 us
  Pallas kernels: 0 us -> 113 us
  matrix products: 37.2 us -> 0 us
  between operations: 14.6 us -> 0.65 us
  local copies, waits for them, and re-layouts: 11.2 us -> 5.07 us
    psum x1 -> x0, waiting for transfers between devices: 147 us -> none  [per_device(): lax.psum(image_part.astype(jnp.bfloat16), 'cuts').astype(jnp.float32)]
    unnamed x5 -> x0, waiting for transfers between devices: 136 us -> none
    pallas_call x0 -> x1, Pallas kernels: none -> 113 us  [per_device(): pl.pallas_call(kernel, out_shape=outs, in_specs=[pl.BlockSpec(memory_spac...]
    reduce_scatter x1 -> x0, waiting for transfers between devices: 65.3 us -> none  [per_device(): lax.psum_scatter(contract_rows(weights, image_vectors).astype(jnp.bfloat1...]
    all_gather x1 -> x0, waiting for transfers between devices: 61.9 us -> none  [per_device(): arrived = lax.all_gather(text_vectors, 'loop', axis=0, tiled=True)]
    dot_general x9 -> x0, matrix products: 37.2 us -> none  [the longest x3 10.5 us: contract_rows(): lax.dot_general(left, right, (((0,), (0,)), ((), ())), preferred_element_...]
    unnamed x28 -> x10, local copies, waits for them, and re-layouts: 11.2 us -> 5.07 us
  transfers between devices with their start and end apart: 4 -> 0, of which waited for: 4 -> 0; matrix products, arithmetic and copies ran while one was open for 4% -> 0% of each run, Pallas kernels for 0% -> 0%
where the time goes in v1:
time: 119 us
  Pallas kernels  113 us (95%)
  local copies, waits for them, and re-layouts  5.07 us (4%)
    pallas_call x1, Pallas kernels, per_device(): pl.pallas_call(kernel, out_shape=outs, in_specs=[pl.BlockSpec(memory_spac...  113 us
    unnamed x10, local copies, waits for them, and re-layouts  5.07 us

profile of v1, /device:TPU:1, one launch (start us, length us, event | category | flops | bytes accessed | tf_op | source)
XLA Modules:
  0.0 118.9 jit_solution(3347182333477743210)
XLA Ops:
  0.6 113.1 %siglip_back.1 = (f32[256,1152]{1,0:T(8,128)}, f32[256,1152]{1,0:T(8,128)}, f32[72,1152]{1,0:T(8,128)}, f32[72,1152]{1,0:T(8,128)}) custom-call(bf16[256,1152]{1,0:T(8,128)(2,1)} %fi_hbm.1, bf16[256,1152]{1,0:T(8,128)(2,1)} %ft_hbm.1, bf16[1152,1152]{1,0:T(8,128)(2,1)} %hi_hbm.1, bf16[1152,1152]{1,0:T(8,128)(2,1)} %ht_hbm.1), custom_call_target="tpu_custom_call" | custom-call | tf_op jit(solution)/shard_map/siglip_back/pallas_call | solution.py:409
  113.8 0.0 copy-start
  113.8 2.5 %copy.12 = f32[256,1152]{1,0:T(8,128)} copy(f32[256,1152]{1,0:T(8,128)} %get-tuple-element.8) | data formatting | bytes 2359296
  116.3 0.0 copy-done
  116.3 0.0 copy-start.2
  116.3 0.0 copy-start.1
  116.3 1.0 copy.13
  117.3 0.1 copy-done.2
  117.4 0.7 copy.14
  118.1 0.0 copy-done.1
  118.1 0.7 copy.15
Async XLA Ops:
  113.8 2.5 %copy-start = (f32[256,1152]{1,0:T(8,128)S(1)}, f32[256,1152]{1,0:T(8,128)}, u32[]{:S(2)}) copy-start(f32[256,1152]{1,0:T(8,128)} %get-tuple-element.9) | copy-start | bytes 3538948
  116.3 1.2 copy-start.2
  116.3 1.9 %copy-start.1 = (f32[72,1152]{1,0:T(8,128)S(1)}, f32[72,1152]{1,0:T(8,128)}, u32[]{:S(2)}) copy-start(f32[72,1152]{1,0:T(8,128)} %get-tuple-element.11) | copy-start | bytes 995332

commit v2 on v0

v2 whole, which is shorter than its diff:
```python
import jax
import jax.numpy as jnp
from jax import lax
from jax.experimental import pallas as pl
from jax.experimental.pallas import tpu as pltpu
from jax.sharding import PartitionSpec as P

SCORE_SCALE = 10.0
SCORE_BIAS = -2.5
EPSILON = 1e-06

D = 1152
B = 256
HB = 128
NZ, NY, NX = 8, 4, 4
BLK = 8
BR = D // BLK
RT, CT = BR // 16, D // 128
NT = RT * CT
ZH = 3
ZT = 2 * ZH
ZN = ZT * NZ
YT = (NT - ZN + 1) // 2
TP = ZN + 2 * YT
YP = 3
YW = YP * NZ
FIN = ZN + 2 * YW
F32, BF16 = jnp.float32, jnp.bfloat16
MESH = pl.DeviceIdType.MESH
NT_DIMS = (((1,), (1,)), ((), ()))
TN_DIMS = (((0,), (0,)), ((), ()))


def kernel(
    fi_hbm, ft_hbm, hi_hbm, ht_hbm,
    gi_hbm, gt_hbm, wi_hbm, wt_hbm,
    fi, ft, hi, ht, x32, xb, sx, y32, yb, sy, w, wt, gi, gt, g2, dpp, dqp,
    gsend, rx_opp, rx_l, rx_r, gysend, gyrecv, ysend, yrecv,
    tt, trecv, zr, zs, yr, ys, ysum, xr, xsum, qr, qg, psum, pr, zg, fin, finr, wi, wo,
    s_loc, s_fi, r_fi, s_ft, r_ft, s_yb, r_yb, s_gx, r_gx, s_gy, r_gy, s_y, r_y,
    s_t, r_t, s_z, r_z, s_yr, r_yr, s_x, r_x, s_q, r_q, s_k, r_k, s_p, r_p, s_g, r_g, s_f, r_f, s_out,
):
    cuts, loop = lax.axis_index("cuts"), lax.axis_index("loop")
    z, yh = cuts // 2, cuts % 2
    yl, x, core = loop // 8, (loop // 2) % 4, loop % 2
    yp = yh * 2 + yl
    me_plane = yp * NX + x

    def dev(z_, yp_, x_, c_):
        return (z_ * 2 + yp_ // 2, ((yp_ % 2) * NX + x_) * 2 + c_)

    xpeer = [dev(z, yp, (x + r) % NX, core) for r in range(NX)]
    ypeer = [dev(z, (yp + r) % NY, x, core) for r in range(NY)]
    zpeer = [dev((z + r) % NZ, yp, x, core) for r in range(NZ)]
    right, left = xpeer[1], xpeer[3]
    mate = dev(z, yh * 2 + 1 - yl, x, core)
    sib = dev(z, yp, x, 1 - core)

    def plane(r):
        q = (me_plane + r) % 16
        return dev(z, q // 4, q % 4, core), q % 8

    def local(src, dst, k):
        c = pltpu.make_async_copy(src, dst, s_loc.at[k])
        c.start()
        return c

    barrier = pltpu.get_barrier_semaphore()
    peers = [sib, right, left, ypeer[1], ypeer[3], zpeer[1], zpeer[7]]
    for p in peers:
        pl.semaphore_signal(barrier, inc=1, device_id=p, device_id_type=MESH)
    l_ft = local(ft_hbm, ft.at[0], 0)
    l_ht = local(ht_hbm, ht, 1)
    l_fi = local(fi_hbm, fi.at[0], 2)
    l_hi = local(hi_hbm, hi, 3)
    pl.semaphore_wait(barrier, len(peers))

    def remote(src, dst, ss, rs, to):
        return pltpu.make_async_remote_copy(
            src_ref=src, dst_ref=dst, send_sem=ss, recv_sem=rs, device_id=to, device_id_type=MESH
        )

    A, Bh = pl.ds(0, HB), pl.ds(HB, HB)
    c_ra = remote(fi_hbm.at[A], fi.at[1, A], s_fi.at[0], r_fi.at[0], right)
    c_lb = remote(fi_hbm.at[Bh], fi.at[1, Bh], s_fi.at[1], r_fi.at[1], left)
    c_rb = remote(fi_hbm.at[Bh], fi.at[2, Bh], s_fi.at[2], r_fi.at[2], right)
    c_la = remote(fi_hbm.at[A], fi.at[2, A], s_fi.at[3], r_fi.at[3], left)
    c_ft = remote(ft_hbm, ft.at[1], s_ft, r_ft, mate)
    c_ra.start()
    c_lb.start()
    c_ft.start()
    c_rb.start()
    c_la.start()
    c_oa = remote(fi.at[1, A], fi.at[3, A], s_fi.at[4], r_fi.at[4], right)
    c_ob = remote(fi.at[1, Bh], fi.at[3, Bh], s_fi.at[5], r_fi.at[5], left)

    def normalize(f, h_ref, v32, vb, s_ref):
        p = jnp.dot(f, h_ref[...], preferred_element_type=F32)
        s = lax.rsqrt(jnp.sum(p * p, axis=-1, keepdims=True) + EPSILON)
        v = p * s
        v32[...] = v
        vb[...] = v.astype(BF16)
        s_ref[...] = s

    place = (0, 2, 1, 3)

    def weigh(i0, m, j0, n):
        dots = lax.dot_general(
            xb[pl.ds(i0, m)].reshape(m * B, D), yb[pl.ds(j0, n)].reshape(n * B, D), NT_DIMS,
            preferred_element_type=F32,
        )
        for i in range(m):
            for j in range(n):
                sc = SCORE_SCALE * dots[i * B : i * B + B, j * B : j * B + B] + SCORE_BIAS
                half = (SCORE_SCALE * 0.5) * jnp.tanh(0.5 * sc)
                val = half + SCORE_SCALE * 0.5
                if i0 + i == 0 and j0 + j == 0:
                    same = lax.broadcasted_iota(jnp.int32, (B, B), 0) == lax.broadcasted_iota(
                        jnp.int32, (B, B), 1
                    )
                    val = jnp.where(same, half - SCORE_SCALE * 0.5, val)
                w[i0 + i, :, pl.ds((j0 + j) * B, B)] = val.astype(BF16)
                wt[place[j0 + j], :, pl.ds((i0 + i) * B, B)] = val.T.astype(BF16)

    def pull(i):
        return jnp.dot(w[i], yb[...].reshape(4 * B, D), preferred_element_type=F32)

    def back(u, s, g):
        return (s * (g - u * jnp.sum(u * g, axis=-1, keepdims=True))).astype(BF16)

    c_yb = [remote(yb.at[2 * k], yb.at[2 * k + 1], s_yb.at[k], r_yb.at[k], sib) for k in range(2)]

    l_ft.wait()
    l_ht.wait()
    normalize(ft[0], ht, y32.at[0], yb.at[0], sy.at[0])
    c_yb[0].start()
    l_fi.wait()
    l_hi.wait()
    normalize(fi[0], hi, x32.at[0], xb.at[0], sx.at[0])
    c_yb[0].wait_recv()
    weigh(0, 1, 0, 2)
    c_ra.wait_recv()
    c_oa.start()
    c_lb.wait_recv()
    c_ob.start()
    normalize(fi[1], hi, x32.at[1], xb.at[1], sx.at[1])
    weigh(1, 1, 0, 2)
    c_ft.wait_recv()
    normalize(ft[1], ht, y32.at[1], yb.at[2], sy.at[1])
    c_yb[1].start()
    c_rb.wait_recv()
    c_la.wait_recv()
    normalize(fi[2], hi, x32.at[2], xb.at[2], sx.at[2])
    weigh(2, 1, 0, 2)
    weigh(0, 3, 2, 1)
    c_yb[1].wait_recv()
    weigh(0, 3, 3, 1)

    def image_pull(i, keep):
        g = pull(i)
        if keep is not None:
            keep[...] = g
        if i:
            gsend[i - 1] = g.astype(BF16)
        dpp[pl.ds(i * B, B)] = back(x32[i], sx[i], g)

    image_pull(1, None)
    c_nb = remote(gsend.at[0, Bh], rx_l.at[Bh], s_gx.at[0], r_gx.at[0], right)
    c_na = remote(gsend.at[0, A], rx_r.at[A], s_gx.at[1], r_gx.at[1], left)
    c_nb.start()
    c_na.start()
    c_oa.wait_recv()
    c_ob.wait_recv()
    normalize(fi[3], hi, x32.at[3], xb.at[3], sx.at[3])
    weigh(3, 1, 0, 4)
    image_pull(3, None)
    c_pa = remote(gsend.at[2, A], rx_opp.at[A], s_gx.at[2], r_gx.at[2], right)
    c_pb = remote(gsend.at[2, Bh], rx_opp.at[Bh], s_gx.at[3], r_gx.at[3], left)
    c_pa.start()
    c_pb.start()

    def text_pull(j0):
        return jnp.dot(
            wt[pl.ds(j0, 2)].reshape(2 * B, 4 * B), xb[...].reshape(4 * B, D),
            preferred_element_type=F32,
        )

    gysend[...] = text_pull(2).astype(BF16)
    c_gy = remote(gysend, gyrecv, s_gy, r_gy, sib)
    c_gy.start()
    image_pull(0, gi)
    image_pull(2, g2)
    gt[...] = text_pull(0)

    thirds = ((0, 2), (2, 3), (5, 3))

    def t_copy(slot, k):
        at = pl.ds(*thirds[k])
        return remote(tt.at[slot, at], trecv.at[at], s_t.at[k], r_t.at[k], sib)

    c_t = [t_copy(0, k) for k in range(3)]
    CH = D // 3

    def head(f_ref, d_ref, slot, sender):
        f = f_ref[...].reshape(-1, D)
        for k in range(3):
            o = lax.dot_general(
                f[:, k * CH : (k + 1) * CH], d_ref[...], TN_DIMS, preferred_element_type=F32
            ).astype(BF16)
            a = 0
            while a < CH // 16:
                b, r = divmod(k * (CH // 16) + a, RT)
                n = min(RT - r, CH // 16 - a)
                for c in range(CT):
                    tt[slot, b, pl.ds(c * RT + r, n)] = o[
                        a * 16 : (a + n) * 16, c * 128 : c * 128 + 128
                    ].reshape(n, 16, 128)
                a += n

            @pl.when(core == sender)
            def _(k=k):
                t_copy(slot, k).start()

    if TP > NT:
        zero = jnp.zeros((BLK, TP - NT, 16, 128), BF16)
        tt[0, :, pl.ds(NT, TP - NT)] = zero
        tt[1, :, pl.ds(NT, TP - NT)] = zero
    head(fi, dpp, 0, 1)
    c_gy.wait_recv()
    g = gt[...] + gyrecv[...].reshape(2 * B, D).astype(F32)
    gt[...] = g
    ysend[...] = g[B:].astype(BF16)
    dqp[...] = back(y32[...].reshape(2 * B, D), sy[...].reshape(2 * B, 1), g)
    head(ft, dqp, 1, 0)

    c_pa.wait_recv()
    c_pb.wait_recv()
    gsend[1] = (g2[...] + rx_opp[...].astype(F32)).astype(BF16)
    c_qa = remote(gsend.at[1, A], rx_l.at[A], s_gx.at[4], r_gx.at[4], right)
    c_qb = remote(gsend.at[1, Bh], rx_r.at[Bh], s_gx.at[5], r_gx.at[5], left)

    for k, (b0, nb) in enumerate(thirds):
        c_t[k].wait_recv()
        for kept in range(2):

            def merge_t(b, _, kept=kept):
                trecv[b] = (tt[kept, b].astype(F32) + trecv[b].astype(F32)).astype(BF16)
                return 0

            @pl.when(core == kept)
            def _(b0=b0, nb=nb, merge_t=merge_t):
                lax.fori_loop(b0, b0 + nb, merge_t, 0)

    def zpiece(d, half, r):
        return pl.ds(ZT * ((z + (r if d == 0 else NZ - r)) % NZ) + ZH * half, ZH)

    order = [[(d, 4)] + [m for r in (3, 2, 1) for m in ((1 - d, r), (d, r))] for d in range(2)]
    cz = [[None] * 7, [None] * 7]

    def z_send(d, k):
        half, r = order[d][k]
        if k < 2:
            src = trecv.at[:, zpiece(d, half, r)]
        else:
            cz[d][k - 2].wait_recv()

            def add(b, _):
                zs[d, k - 2, b] = (
                    trecv[b, zpiece(d, half, r)].astype(F32) + zr[d, k - 2, b].astype(F32)
                ).astype(BF16)
                return 0

            lax.fori_loop(0, BLK, add, 0)
            src = zs.at[d, k - 2]
        cz[d][k] = remote(src, zr.at[d, k], s_z.at[d, k], r_z.at[d, k], zpeer[1 if d == 0 else 7])
        cz[d][k].start()

    def ypiece(r, half):
        t = (yp + r) % NY
        return pl.ds(4 * (t % 2) + 2 * half, 2), pl.ds(ZN + YT * (t // 2), YT)

    cy = [[None] * 3, [None] * 3]

    def y_send(d, k):
        to = ypeer[1 if d == 0 else 3]
        half = d if k != 1 else 1 - d
        bs, ts = ypiece(2 if k == 0 else (1 if d == 0 else 3), half)
        src = trecv.at[bs, ts]
        if k == 2:
            cy[d][0].wait_recv()
            ys[d] = (trecv[bs, ts].astype(F32) + yr[d, 0].astype(F32)).astype(BF16)
            src = ys.at[d]
        cy[d][k] = remote(src, yr.at[d, k], s_yr.at[d, k], r_yr.at[d, k], to)
        cy[d][k].start()

    for k in range(2):
        for d in range(2):
            z_send(d, k)
            y_send(d, k)
    c_qa.start()
    c_qb.start()
    z_send(0, 2)
    z_send(1, 2)
    y_send(0, 2)
    y_send(1, 2)
    for k in (3, 4, 5):
        z_send(0, k)
        z_send(1, k)
    for half, parts in ((0, ((0, 2), (1, 1))), (1, ((0, 1), (1, 2)))):
        bs, ts = ypiece(0, half)
        v = trecv[bs, ts].astype(F32)
        for d, k in parts:
            cy[d][k].wait_recv()
            v += yr[d, k].astype(F32)
        ysum[pl.ds(2 * half, 2)] = v.astype(BF16)
    c_x = []
    for r in range(1, NX):
        c_x.append(remote(ysum.at[(x + r) % NX], xr.at[r], s_x.at[r], r_x.at[r], xpeer[r]))
        c_x[-1].start()
    c_y = remote(ysend, yrecv, s_y, r_y, mate)
    c_y.start()
    z_send(0, 6)
    z_send(1, 6)
    v = ysum[x].astype(F32)
    for r in range(1, NX):
        c_x[r - 1].wait_recv()
        v += xr[r].astype(F32)
    xsum[pl.ds(0, YT)] = v.astype(BF16)
    xsum[pl.ds(YT, YW - YT)] = jnp.zeros((YW - YT, 16, 128), BF16)
    c_q = []
    for r in range(1, NZ):
        c_q.append(
            remote(xsum.at[pl.ds(YP * ((z + r) % NZ), YP)], qr.at[r], s_q.at[r], r_q.at[r], zpeer[r])
        )
        c_q[-1].start()
    for half, parts in ((0, ((0, 6), (1, 5))), (1, ((0, 5), (1, 6)))):
        for d, k in parts:
            cz[d][k].wait_recv()

        def own(b, _, half=half, parts=parts):
            v = trecv[b, zpiece(0, half, 0)].astype(F32)
            for d, k in parts:
                v += zr[d, k, b].astype(F32)
            psum[b, pl.ds(ZH * half, ZH)] = v.astype(BF16)
            return 0

        lax.fori_loop(0, BLK, own, 0)
    c_p = []
    for r in range(1, 16):
        to, blk = plane(r)
        c_p.append(remote(psum.at[blk], pr.at[r], s_p.at[r], r_p.at[r], to))
        c_p[-1].start()
    pr[0] = psum[me_plane % 8]
    v = xsum[pl.ds(YP * z, YP)].astype(F32)
    for r in range(1, NZ):
        c_q[r - 1].wait_recv()
        v += qr[r].astype(F32)
    qg[0] = v.astype(BF16)
    c_k = []
    for r in range(1, 16):
        dz, dy = r % 8, r // 8
        to = dev((z + dz) % NZ, (yp + 2 * dy) % NY, x, core)
        c_k.append(remote(qg.at[0], qg.at[r], s_k.at[r], r_k.at[r], to))
        c_k[-1].start()
    for c in c_p:
        c.wait_recv()
    total = pr[me_plane].astype(F32)
    for q in range(1, 16):
        total += pr[(me_plane + 16 - q) % 16].astype(F32)
    zg[0] = total.astype(BF16)
    c_g = []
    for r in range(1, NZ):
        c_g.append(remote(zg.at[0], zg.at[r], s_g.at[r], r_g.at[r], zpeer[r]))
        c_g[-1].start()

    outs = []

    def put(src, dst):
        outs.append(pltpu.make_async_copy(src, dst, s_out.at[len(outs)]))
        outs[-1].start()

    for c in (c_nb, c_na, c_qa, c_qb):
        c.wait_recv()
    dpf = back(x32[0], sx[0], gi[...] + rx_l[...].astype(F32) + rx_r[...].astype(F32))
    gi[...] = lax.dot_general(dpf, hi[...], NT_DIMS, preferred_element_type=F32)
    put(gi, gi_hbm)
    c_y.wait_recv()
    dqf = back(y32[0], sy[0], gt[pl.ds(0, B)] + yrecv[...].astype(F32))
    gt[pl.ds(0, B)] = lax.dot_general(dqf, ht[...], NT_DIMS, preferred_element_type=F32)
    put(gt.at[pl.ds(0, B)], gt_hbm)

    fin[pl.ds(ZN + YW * yh + YP * z, YP)] = qg[0]
    for r in range(1, 16):
        dz, dy = r % 8, r // 8
        c_k[r - 1].wait_recv()
        fin[pl.ds(ZN + YW * ((yh + dy) % 2) + YP * ((z + NZ - dz) % NZ), YP)] = qg[r]
    rest, front = pl.ds(ZN, FIN - ZN), pl.ds(0, ZN)
    c_fr = remote(fin.at[rest], finr.at[rest], s_f.at[0], r_f.at[0], sib)
    c_fr.start()
    fin[pl.ds(ZT * z, ZT)] = zg[0]
    for r in range(1, NZ):
        c_g[r - 1].wait_recv()
        fin[pl.ds(ZT * ((z + NZ - r) % NZ), ZT)] = zg[r]
    c_ff = remote(fin.at[front], finr.at[front], s_f.at[1], r_f.at[1], sib)
    c_ff.start()

    def emit(ref, out, first):
        def place_of(t):
            return t if t < ZN else ZN + YW * ((t - ZN) // YT) + (t - ZN) % YT

        r0, r1 = first // 16, -(-(first + BR // 2) // 16)
        for c in range(CT):
            r = r0
            while r < r1:
                t, n = place_of(c * RT + r), 1
                while r + n < r1 and place_of(c * RT + r + n) == t + n:
                    n += 1
                lo, up_ = max(r * 16, first), min((r + n) * 16, first + BR // 2)
                rows = ref[pl.ds(t, n)].astype(F32).reshape(n * 16, 128)
                out[pl.ds(lo - first, up_ - lo), pl.ds(c * 128, 128)] = rows[
                    lo - r * 16 : up_ - r * 16
                ]
                r += n

    @pl.when(core == 0)
    def _():
        emit(fin, wi, 0)
        c_fr.wait_recv()
        c_ff.wait_recv()
        emit(finr, wo, 0)

    @pl.when(core == 1)
    def _():
        emit(fin, wo, BR // 2)
        c_fr.wait_recv()
        c_ff.wait_recv()
        emit(finr, wi, BR // 2)

    put(wi, wi_hbm)
    put(wo, wt_hbm)
    for c in (
        [c_ra, c_rb, c_lb, c_la, c_ft, c_oa, c_ob, c_nb, c_na, c_pa, c_pb, c_qa, c_qb, c_gy, c_y]
        + c_yb + c_t + cz[0] + cz[1] + cy[0] + cy[1] + c_x + c_q + c_p + c_k + c_g + [c_fr, c_ff]
    ):
        c.wait_send()
    for c in outs:
        c.wait()


def hand_on(*refs):
    ins, outs, bufs, sem_in, sem_out = refs[:4], refs[4:8], refs[8:12], refs[12], refs[13]
    parts = []
    for a, o, v in zip(ins, outs, bufs):
        n = 2 if a.shape[0] == B else 1
        rows = a.shape[0] // n
        for k in range(n):
            at = pl.ds(k * rows, rows)
            parts.append(
                (
                    pltpu.make_async_copy(a.at[at], v.at[at], sem_in.at[len(parts)]),
                    pltpu.make_async_copy(v.at[at], o.at[at], sem_out.at[len(parts)]),
                )
            )
    for c, _ in parts:
        c.start()
    for c, d in parts:
        c.wait()
        d.start()
    for _, d in parts:
        d.wait()


def per_device(image_features, text_features, image_head, text_head):
    vm, dma = pltpu.VMEM, pltpu.SemaphoreType.DMA
    outs = (
        jax.ShapeDtypeStruct((B, D), F32),
        jax.ShapeDtypeStruct((B, D), F32),
        jax.ShapeDtypeStruct((BR // 2, D), F32),
        jax.ShapeDtypeStruct((BR // 2, D), F32),
    )
    tile = (16, 128)
    got = pl.pallas_call(
        kernel,
        out_shape=outs,
        in_specs=[pl.BlockSpec(memory_space=pl.ANY)] * 4,
        out_specs=[pl.BlockSpec(memory_space=pl.ANY)] * 4,
        scratch_shapes=[
            vm((4, B, D), BF16), vm((2, B, D), BF16), vm((D, D), BF16), vm((D, D), BF16),
            vm((4, B, D), F32), vm((4, B, D), BF16), vm((4, B, 1), F32),
            vm((2, B, D), F32), vm((4, B, D), BF16), vm((2, B, 1), F32),
            vm((4, B, 4 * B), BF16), vm((4, B, 4 * B), BF16),
            vm((B, D), F32), vm((2 * B, D), F32), vm((B, D), F32),
            vm((4 * B, D), BF16), vm((2 * B, D), BF16),
            vm((3, B, D), BF16), vm((B, D), BF16), vm((B, D), BF16), vm((B, D), BF16),
            vm((2 * B, D), BF16), vm((2 * B, D), BF16),
            vm((B, D), BF16), vm((B, D), BF16),
            vm((2, BLK, TP) + tile, BF16), vm((BLK, TP) + tile, BF16),
            vm((2, 7, BLK, ZH) + tile, BF16), vm((2, 5, BLK, ZH) + tile, BF16),
            vm((2, 3, 2, YT) + tile, BF16), vm((2, 2, YT) + tile, BF16),
            vm((4, YT) + tile, BF16), vm((4, YT) + tile, BF16),
            vm((YW,) + tile, BF16), vm((NZ, YP) + tile, BF16), vm((16, YP) + tile, BF16),
            vm((BLK, ZT) + tile, BF16), vm((16, ZT) + tile, BF16), vm((NZ, ZT) + tile, BF16),
            vm((FIN,) + tile, BF16), vm((FIN,) + tile, BF16),
            vm((BR // 2, D), F32), vm((BR // 2, D), F32),
            dma((4,)), dma((6,)), dma((6,)), dma(()), dma(()), dma((2,)), dma((2,)),
            dma((6,)), dma((6,)), dma(()), dma(()), dma(()), dma(()),
            dma((3,)), dma((3,)), dma((2, 7)), dma((2, 7)), dma((2, 3)), dma((2, 3)),
            dma((4,)), dma((4,)), dma((8,)), dma((8,)), dma((16,)), dma((16,)), dma((16,)), dma((16,)),
            dma((8,)), dma((8,)), dma((2,)), dma((2,)), dma((4,)),
        ],
        compiler_params=pltpu.CompilerParams(
            collective_id=0, has_side_effects=True, vmem_limit_bytes=63 << 20
        ),
        name="siglip_back",
    )(image_features, text_features, image_head, text_head)
    return pl.pallas_call(
        hand_on,
        out_shape=outs,
        in_specs=[pl.BlockSpec(memory_space=pl.ANY)] * 4,
        out_specs=[pl.BlockSpec(memory_space=pl.ANY)] * 4,
        scratch_shapes=[vm(o.shape, F32) for o in outs] + [dma((6,)), dma((6,))],
        name="hand_on",
    )(*got)


def solution(mesh):
    placed = (P(("cuts", "loop"), None), P(("cuts", "loop"), None), P(), P())
    return jax.shard_map(
        per_device,
        mesh=mesh,
        in_specs=placed,
        out_specs=(
            P(("cuts", "loop"), None),
            P(("cuts", "loop"), None),
            P("loop", None),
            P("loop", None),
        ),
        check_vma=False,
    )
```

time: 487 us -> 91.2 us (0.19); the launches traced: 477 us -> 91.1 us
  waiting for transfers between devices: 410 us -> 0 us
  Pallas kernels: 0 us -> 90.3 us
  matrix products: 37.2 us -> 0 us
  between operations: 14.6 us -> 0.8 us
  local copies, waits for them, and re-layouts: 11.2 us -> 0 us
    psum x1 -> x0, waiting for transfers between devices: 147 us -> none  [per_device(): lax.psum(image_part.astype(jnp.bfloat16), 'cuts').astype(jnp.float32)]
    unnamed x5 -> x0, waiting for transfers between devices: 136 us -> none
    pallas_call x0 -> x2, Pallas kernels: none -> 90.3 us  [the longest x1 87.5 us: per_device(): pl.pallas_call(kernel, out_shape=outs, in_specs=[pl.BlockSpec(memory_spac...]
    reduce_scatter x1 -> x0, waiting for transfers between devices: 65.3 us -> none  [per_device(): lax.psum_scatter(contract_rows(weights, image_vectors).astype(jnp.bfloat1...]
    all_gather x1 -> x0, waiting for transfers between devices: 61.9 us -> none  [per_device(): arrived = lax.all_gather(text_vectors, 'loop', axis=0, tiled=True)]
    dot_general x9 -> x0, matrix products: 37.2 us -> none  [the longest x3 10.5 us: contract_rows(): lax.dot_general(left, right, (((0,), (0,)), ((), ())), preferred_element_...]
    unnamed x28 -> x0, local copies, waits for them, and re-layouts: 11.2 us -> none
  transfers between devices with their start and end apart: 4 -> 0, of which waited for: 4 -> 0; matrix products, arithmetic and copies ran while one was open for 4% -> 0% of each run, Pallas kernels for 0% -> 0%
where the time goes in v2:
time: 91.2 us; the launch traced here: 91.1 us
  Pallas kernels  90.3 us (99%)
    pallas_call x1, Pallas kernels, per_device(): pl.pallas_call(kernel, out_shape=outs, in_specs=[pl.BlockSpec(memory_spac...  87.5 us
    pallas_call x1, Pallas kernels, per_device(): pl.pallas_call(hand_on, out_shape=outs, in_specs=[pl.BlockSpec(memory_spa...  2.78 us

profile of v2, /device:TPU:1, one launch (start us, length us, event | category | flops | bytes accessed | tf_op | source)
XLA Modules:
  0.0 91.1 jit_solution(7375716347874148082)
XLA Ops:
  0.6 87.5 %siglip_back.1 = (f32[256,1152]{1,0:T(8,128)}, f32[256,1152]{1,0:T(8,128)}, f32[72,1152]{1,0:T(8,128)}, f32[72,1152]{1,0:T(8,128)}) custom-call(bf16[256,1152]{1,0:T(8,128)(2,1)} %fi_hbm.1, bf16[256,1152]{1,0:T(8,128)(2,1)} %ft_hbm.1, bf16[1152,1152]{1,0:T(8,128)(2,1)} %hi_hbm.1, bf16[1152,1152]{1,0:T(8,128)(2,1)} %ht_hbm.1), custom_call_target="tpu_custom_call" | custom-call | tf_op jit(solution)/shard_map/siglip_back/pallas_call | solution.py:482
  88.1 2.8 %hand_on.1 = (f32[256,1152]{1,0:T(8,128)}, f32[256,1152]{1,0:T(8,128)}, f32[72,1152]{1,0:T(8,128)}, f32[72,1152]{1,0:T(8,128)}) custom-call(f32[256,1152]{1,0:T(8,128)} %get-tuple-element.8.refs_0_, f32[256,1152]{1,0:T(8,128)} %get-tuple-element.9.refs_1_, f32[72,1152]{1,0:T(8,128)} %get-tuple-element.10.refs_2_, f32[72,1152]{1,0:T(8,128)} %get-tuple-element.11.refs_3_), custom_call_target="tpu_custom_call" | custom-call | tf_op jit(solution)/shard_map/hand_on/pallas_call | solution.py:516

commit v3 on v2

--- a/solution.py
+++ b/solution.py
@@ -169,6 +169,8 @@
     c_na = remote(gsend.at[0, A], rx_r.at[A], s_gx.at[1], r_gx.at[1], left)
     c_nb.start()
     c_na.start()
+    image_pull(0, gi)
+    image_pull(2, g2)
     c_oa.wait_recv()
     c_ob.wait_recv()
     normalize(fi[3], hi, x32.at[3], xb.at[3], sx.at[3])
@@ -188,8 +190,6 @@
     gysend[...] = text_pull(2).astype(BF16)
     c_gy = remote(gysend, gyrecv, s_gy, r_gy, sib)
     c_gy.start()
-    image_pull(0, gi)
-    image_pull(2, g2)
     gt[...] = text_pull(0)
 
     thirds = ((0, 2), (2, 3), (5, 3))
@@ -233,11 +233,6 @@
     dqp[...] = back(y32[...].reshape(2 * B, D), sy[...].reshape(2 * B, 1), g)
     head(ft, dqp, 1, 0)
 
-    c_pa.wait_recv()
-    c_pb.wait_recv()
-    gsend[1] = (g2[...] + rx_opp[...].astype(F32)).astype(BF16)
-    c_qa = remote(gsend.at[1, A], rx_l.at[A], s_gx.at[4], r_gx.at[4], right)
-    c_qb = remote(gsend.at[1, Bh], rx_r.at[Bh], s_gx.at[5], r_gx.at[5], left)
 
     for k, (b0, nb) in enumerate(thirds):
         c_t[k].wait_recv()
@@ -297,13 +292,18 @@
         for d in range(2):
             z_send(d, k)
             y_send(d, k)
+    c_pa.wait_recv()
+    c_pb.wait_recv()
+    gsend[1] = (g2[...] + rx_opp[...].astype(F32)).astype(BF16)
+    c_qa = remote(gsend.at[1, A], rx_l.at[A], s_gx.at[4], r_gx.at[4], right)
+    c_qb = remote(gsend.at[1, Bh], rx_r.at[Bh], s_gx.at[5], r_gx.at[5], left)
     c_qa.start()
     c_qb.start()
     z_send(0, 2)
     z_send(1, 2)
     y_send(0, 2)
     y_send(1, 2)
-    for k in (3, 4, 5):
+    for k in (3, 4):
         z_send(0, k)
         z_send(1, k)
     for half, parts in ((0, ((0, 2), (1, 1))), (1, ((0, 1), (1, 2)))):
@@ -317,6 +317,8 @@
     for r in range(1, NX):
         c_x.append(remote(ysum.at[(x + r) % NX], xr.at[r], s_x.at[r], r_x.at[r], xpeer[r]))
         c_x[-1].start()
+    z_send(0, 5)
+    z_send(1, 5)
     c_y = remote(ysend, yrecv, s_y, r_y, mate)
     c_y.start()
     z_send(0, 6)
@@ -451,7 +453,7 @@
     ins, outs, bufs, sem_in, sem_out = refs[:4], refs[4:8], refs[8:12], refs[12], refs[13]
     parts = []
     for a, o, v in zip(ins, outs, bufs):
-        n = 2 if a.shape[0] == B else 1
+        n = 4 if a.shape[0] == B else 1
         rows = a.shape[0] // n
         for k in range(n):
             at = pl.ds(k * rows, rows)
@@ -518,7 +520,7 @@
         out_shape=outs,
         in_specs=[pl.BlockSpec(memory_space=pl.ANY)] * 4,
         out_specs=[pl.BlockSpec(memory_space=pl.ANY)] * 4,
-        scratch_shapes=[vm(o.shape, F32) for o in outs] + [dma((6,)), dma((6,))],
+        scratch_shapes=[vm(o.shape, F32) for o in outs] + [dma((10,)), dma((10,))],
         name="hand_on",
     )(*got)
 

time: 91.2 us -> 91 us (level)
  no operation moved by 1% of the time
where the time goes in v3:
time: 91 us; the launch traced here: 90.6 us
  Pallas kernels  89.8 us (99%)
    pallas_call x1, Pallas kernels, per_device(): pl.pallas_call(kernel, out_shape=outs, in_specs=[pl.BlockSpec(memory_spac...  87.1 us
    pallas_call x1, Pallas kernels, per_device(): pl.pallas_call(hand_on, out_shape=outs, in_specs=[pl.BlockSpec(memory_spa...  2.75 us

profile of v3, /device:TPU:1, one launch (start us, length us, event | category | flops | bytes accessed | tf_op | source)
XLA Modules:
  0.0 90.6 jit_solution(10316954785922181539)
XLA Ops:
  0.6 87.1 %siglip_back.1 = (f32[256,1152]{1,0:T(8,128)}, f32[256,1152]{1,0:T(8,128)}, f32[72,1152]{1,0:T(8,128)}, f32[72,1152]{1,0:T(8,128)}) custom-call(bf16[256,1152]{1,0:T(8,128)(2,1)} %fi_hbm.1, bf16[256,1152]{1,0:T(8,128)(2,1)} %ft_hbm.1, bf16[1152,1152]{1,0:T(8,128)(2,1)} %hi_hbm.1, bf16[1152,1152]{1,0:T(8,128)(2,1)} %ht_hbm.1), custom_call_target="tpu_custom_call" | custom-call | tf_op jit(solution)/shard_map/siglip_back/pallas_call | solution.py:484
  87.7 2.8 %hand_on.1 = (f32[256,1152]{1,0:T(8,128)}, f32[256,1152]{1,0:T(8,128)}, f32[72,1152]{1,0:T(8,128)}, f32[72,1152]{1,0:T(8,128)}) custom-call(f32[256,1152]{1,0:T(8,128)} %get-tuple-element.8.refs_0_, f32[256,1152]{1,0:T(8,128)} %get-tuple-element.9.refs_1_, f32[72,1152]{1,0:T(8,128)} %get-tuple-element.10.refs_2_, f32[72,1152]{1,0:T(8,128)} %get-tuple-element.11.refs_3_), custom_call_target="tpu_custom_call" | custom-call | tf_op jit(solution)/shard_map/hand_on/pallas_call | solution.py:518
